TPU v7x, 512 devices: a whole 4x8x8 slice. The times are simulated.
512 devices in a mesh: dp: 32 (over y, x), col: 16 (over z, core).
Axes of the slice: x: 4, y: 8, z: 8, core: 2. Of those that a mesh axis runs over, the one named last changes fastest.
Arguments:
- source_feats: bfloat16 [768, 131072], P('col', 'dp'), may hold values from -6 to 6
- neighbours: int32 [65536, 25], P('dp'), may hold values from 0 to 4095
- degree: int32 [65536], P('dp'), may hold values from 0 to 25
- counts: int32 [32], P('dp'), may hold values from 256 to 2048, as said below
- upstream: bfloat16 [65536, 1024], P(('dp', 'col')), may hold values from -6 to 6
- preact: bfloat16 [65536, 1024], P(('dp', 'col')), may hold values from -6 to 6
Outputs:
- grad_self: float32 [768, 1024], P('col')
- grad_neigh: float32 [768, 1024], P('col')
- grad_bias: float32 [1024], replicated
Inputs may be any that keep to these rules, and one draw needn't show every extreme that they name: `neighbours`: each dp block's neighbour indices point into that block's 4096 sources. `counts`: some dp index owns all 2048 slots in every draw.
All inputs are finite; a program needn't handle non-finite values.
Results may differ from a plain program's by a relative error of at most 0.0026.
Values may be sent and summed in bfloat16 or wider, within the bound.
A program may use at most 64 MiB of HBM per device.

v0:
```python
import jax
import jax.numpy as jnp
from jax import lax
from jax.sharding import PartitionSpec as P


def aggregate(source_cols, neighbours, degree):
    t_dev, fanout = neighbours.shape
    sources = source_cols.shape[1]
    width = min(512, t_dev)
    blocks = t_dev // width

    def one_block(operands):
        index, deg = operands
        live_slot = lax.broadcasted_iota(jnp.int32, (width, fanout), 1) < deg[:, None]
        src_ids = lax.broadcasted_iota(jnp.int32, (sources, width, fanout), 0)
        hits = (src_ids == index[None, :, :]) & live_slot[None, :, :]
        tally = jnp.sum(hits.astype(jnp.float32), axis=2).astype(jnp.bfloat16)
        total = jnp.dot(source_cols, tally, preferred_element_type=jnp.float32)
        return (total / jnp.maximum(deg, 1).astype(jnp.float32)[None, :]).astype(jnp.bfloat16)

    result = lax.map(
        one_block, (neighbours.reshape(blocks, width, fanout), degree.reshape(blocks, width))
    )
    return jnp.transpose(result, (1, 0, 2)).reshape(source_cols.shape[0], t_dev)


def per_device(source_feats, neighbours, degree, counts, upstream, preact):
    t_dev = neighbours.shape[0]
    row_count = upstream.shape[0]
    limit = counts[0]
    row_ids = lax.axis_index("col") * row_count + lax.broadcasted_iota(jnp.int32, (row_count,), 0)
    keep = (preact > 0) & (row_ids < limit)[:, None]
    dz = jnp.where(keep, upstream, jnp.zeros_like(upstream))
    self_feats = source_feats[:, :t_dev]
    agg = aggregate(source_feats, neighbours, degree)
    scale = jnp.float32(1.0) / jnp.sqrt(jnp.float32(t_dev * lax.axis_size("dp")))
    piece = lax.all_gather(dz, "col", axis=0, tiled=True)
    summed_self, summed_neigh = lax.psum(
        (
            jnp.dot(self_feats, piece, preferred_element_type=jnp.float32),
            jnp.dot(agg, piece, preferred_element_type=jnp.float32),
        ),
        "dp",
    )
    local_bias = jnp.sum(dz.astype(jnp.float32), axis=0)
    summed_bias = lax.psum(local_bias, ("dp", "col"))
    return (summed_self * scale, summed_neigh * scale, summed_bias * scale)


def solution(mesh):
    placed = (
        P("col", "dp"),
        P("dp", None),
        P("dp"),
        P("dp"),
        P(("dp", "col"), None),
        P(("dp", "col"), None),
    )
    return jax.shard_map(
        per_device,
        mesh=mesh,
        in_specs=placed,
        out_specs=(P("col", None), P("col", None), P()),
        check_vma=False,
    )
```

profile of v0, /device:TPU:1, one launch (start us, length us, event | category | flops | bytes accessed | tf_op | source)
XLA Modules:
  0.0 523.9 jit_solution(14889767388497177864)
XLA Ops:
  7.2 0.0 all-gather.2.cloned.1.call-start
  7.9 1.9 convert_reduce_fusion.1
  9.8 0.0 all-gather.2.cloned.1.call-update
  9.8 0.0 all-reduce.3.cloned.1.call-start
  9.9 0.7 reshape.39
  10.6 1.1 reshape.38
  11.7 340.5 %while.10 = (s32[]{:T(128)}, bf16[4,48,512]{2,1,0:T(8,128)(2,1)S(1)}, s32[4,512,25]{1,0,2:T(4,128)S(1)}, s32[4,512]{1,0:T(4,128)S(1)}, bf16[48,4096]{1,0:T(8,128)(2,1)}, /*index=5*/s32[]{:T(128)}) while((s32[]{:T(128)}, bf16[4,48,512]{2,1,0:T(8,128)(2,1)S(1)}, s32[4,512,25]{1,0,2:T(4,128)S(1)}, s32[4,512]{1,0:T(4,128)S(1)}, ...), condition=%wide.region_3.4_spmd, body=%wide.region_1.3_spmd.sunk | while | flops 409007616 | bytes 10695797 | solution.py:22
  11.7 0.0 copy-start.1
  11.7 0.1 constant_dynamic-slice_fusion.4
  11.8 82.0 %convert_reduce_fusion.3 = bf16[4096,512]{1,0:T(8,128)(2,1)} fusion(s32[512,25]{0,1:T(8,128)S(1)} %bitcast.37, pred[512,25]{0,1:T(8,128)(4,1)S(1)} %iota_compare_fusion.3), kind=kLoop, calls=%fused_computation.clone.1 | loop fusion | flops 207618048 | bytes 4258304 | tf_op jit(solution)/shard_map/while/body/eval_jaxpr/reduce_sum | solution.py:18
  93.8 0.0 copy-done.1
  93.8 3.0 fusion.27
  96.8 0.0 copy-start.1
  96.9 0.1 constant_dynamic-slice_fusion.4
  96.9 82.0 %convert_reduce_fusion.3 = bf16[4096,512]{1,0:T(8,128)(2,1)} fusion(s32[512,25]{0,1:T(8,128)S(1)} %bitcast.37, pred[512,25]{0,1:T(8,128)(4,1)S(1)} %iota_compare_fusion.3), kind=kLoop, calls=%fused_computation.clone.1 | loop fusion | flops 207618048 | bytes 4258304 | tf_op jit(solution)/shard_map/while/body/eval_jaxpr/reduce_sum | solution.py:18
  178.9 0.0 copy-done.1
  178.9 3.0 fusion.27
  181.9 0.0 copy-start.1
  182.0 0.1 constant_dynamic-slice_fusion.4
  182.1 82.0 %convert_reduce_fusion.3 = bf16[4096,512]{1,0:T(8,128)(2,1)} fusion(s32[512,25]{0,1:T(8,128)S(1)} %bitcast.37, pred[512,25]{0,1:T(8,128)(4,1)S(1)} %iota_compare_fusion.3), kind=kLoop, calls=%fused_computation.clone.1 | loop fusion | flops 207618048 | bytes 4258304 | tf_op jit(solution)/shard_map/while/body/eval_jaxpr/reduce_sum | solution.py:18
  264.0 0.0 copy-done.1
  264.0 3.0 fusion.27
  267.1 0.0 copy-start.1
  267.1 0.1 constant_dynamic-slice_fusion.4
  267.2 82.0 %convert_reduce_fusion.3 = bf16[4096,512]{1,0:T(8,128)(2,1)} fusion(s32[512,25]{0,1:T(8,128)S(1)} %bitcast.37, pred[512,25]{0,1:T(8,128)(4,1)S(1)} %iota_compare_fusion.3), kind=kLoop, calls=%fused_computation.clone.1 | loop fusion | flops 207618048 | bytes 4258304 | tf_op jit(solution)/shard_map/while/body/eval_jaxpr/reduce_sum | solution.py:18
  349.2 0.0 copy-done.1
  349.2 3.0 fusion.27
  352.2 0.0 all-gather.2.cloned.1.call-done
  352.2 0.0 copy-start
  352.2 4.0 convolution_bitcast_fusion
  356.2 0.0 copy-done
  356.2 1.5 fusion.16
  357.7 0.0 all-reduce.3.cloned.1.call-update
  357.7 107.6 %psum.23 = f32[1024]{0:T(1024)S(1)} all-reduce(f32[1024]{0:T(1024)S(1)} %get-tuple-element.55), channel_id=1, replica_groups=mesh['dp'=32,'col'=16] {'dp','col'}, use_global_device_ids=true, to_apply=%region_6.7 | all-reduce | flops 1024 | bytes 8192 | tf_op jit(solution)/shard_map/psum | solution.py:47
  465.3 0.6 broadcast_multiply_fusion.2
  465.9 49.3 %all-reduce.3.cloned.1.call-done = (f32[48,1024]{1,0:T(8,128)}, f32[48,1024]{1,0:T(8,128)}) async-done(((f32[48,1024]{1,0:T(8,128)}, f32[48,1024]{1,0:T(8,128)}), (f32[48,1024]{1,0:T(8,128)}, f32[48,1024]{1,0:T(8,128)})) %all-reduce.3.cloned.1.call-update) | async-done | bytes 393232 | tf_op jit(solution)/shard_map/psum | solution.py:39
  515.2 1.8 broadcast_multiply_fusion
  (15 shorter events, 0.1 us)
Async XLA Ops:
  7.2 345.1 %all-gather.2.cloned.1.call-start = ((), (), s32[]{:S(2)}) async-start(), calls=%async_computation | async-start | bytes 4456448 | tf_op jit(solution)/shard_map/all_gather | solution.py:38
  9.8 505.4 %all-reduce.3.cloned.1.call-start = ((), (), s32[]{:S(2)}) async-start(), calls=%async_computation.1 | async-start | bytes 786432 | tf_op jit(solution)/shard_map/psum | solution.py:39
  11.7 82.1 %copy-start.1 = (bf16[48,4096]{1,0:T(8,128)(2,1)S(1)}, bf16[48,4096]{1,0:T(8,128)(2,1)}, u32[]{:S(2)}) copy-start(bf16[48,4096]{1,0:T(8,128)(2,1)} %get-tuple-element.110) | copy-start | bytes 1179652 | tf_op jit(solution)/shard_map/while
  96.8 82.1 %copy-start.1 = (bf16[48,4096]{1,0:T(8,128)(2,1)S(1)}, bf16[48,4096]{1,0:T(8,128)(2,1)}, u32[]{:S(2)}) copy-start(bf16[48,4096]{1,0:T(8,128)(2,1)} %get-tuple-element.110) | copy-start | bytes 1179652 | tf_op jit(solution)/shard_map/while
  181.9 82.1 %copy-start.1 = (bf16[48,4096]{1,0:T(8,128)(2,1)S(1)}, bf16[48,4096]{1,0:T(8,128)(2,1)}, u32[]{:S(2)}) copy-start(bf16[48,4096]{1,0:T(8,128)(2,1)} %get-tuple-element.110) | copy-start | bytes 1179652 | tf_op jit(solution)/shard_map/while
  267.1 82.1 %copy-start.1 = (bf16[48,4096]{1,0:T(8,128)(2,1)S(1)}, bf16[48,4096]{1,0:T(8,128)(2,1)}, u32[]{:S(2)}) copy-start(bf16[48,4096]{1,0:T(8,128)(2,1)} %get-tuple-element.110) | copy-start | bytes 1179652 | tf_op jit(solution)/shard_map/while
  352.2 4.0 copy-start
Sparse Core Ops, SparseCore 0:
  10.1 51.5 all-gather.1
  357.9 157.3 all-reduce.2
where the time goes:
time: 527 us; the launch traced here: 524 us
  other arithmetic  332 us (63%)
  blocking collectives  108 us (20%)
  waiting for transfers between devices  49.4 us (9%)
  matrix products  17.5 us (3%)
  between operations  14.7 us (3%)
    reduce_sum x4, other arithmetic, one_block(): tally = jnp.sum(hits.astype(jnp.float32), axis=2).astype(jnp.bfloat16)  328 us
    psum x1, blocking collectives, per_device(): summed_bias = lax.psum(local_bias, ('dp', 'col'))  108 us
    psum x1, waiting for transfers between devices, per_device(): lax.psum((jnp.dot(self_feats, piece, preferred_element_type=jnp.float32),...  49.3 us
    dot_general x4, matrix products, one_block(): total = jnp.dot(source_cols, tally, preferred_element_type=jnp.float32)  12 us
  transfers between devices with their start and end apart: 2, of which 1 were waited for; matrix products, arithmetic and copies ran while one was open for 65% of the time, Pallas kernels for 0%

commit v1 on v0

v1 whole, which is shorter than its diff:
```python
import jax
import jax.numpy as jnp
from jax import lax
from jax.experimental import pallas as pl
from jax.experimental.pallas import tpu as pltpu
from jax.sharding import PartitionSpec as P

MESH = pl.DeviceIdType.MESH
NT = (((1,), (1,)), ((), ()))
NZ, NY, NX = 8, 8, 4
NDP, NCOL = NY * NX, NZ * 2
C = 2
H = 1024
W = H // C
ROWS = 128
T = 2048
F = 48
NP = NDP - 1


def encode(nbr_ref, deg_ref, hi_s, lo_s):
    k, t = nbr_ref.shape
    nb = nbr_ref[...]
    live = lax.broadcasted_iota(jnp.int32, (k, t), 0) < deg_ref[...]
    j = lax.broadcasted_iota(jnp.int32, (k, t), 1) // 256
    hi = jnp.where(live, (nb >> 8) * 8 + j, 255).astype(jnp.float32)
    lo = (nb & 255).astype(jnp.float32)
    pad = jnp.full((32 - k, t), 255.0, jnp.float32)
    for code, out in ((hi, hi_s), (lo, lo_s)):
        code = jnp.concatenate([code, pad], axis=0)
        out[...] = jnp.concatenate([code[:, i * 256 : (i + 1) * 256] for i in range(8)], axis=0).T


def tally(hi_s, lo_s, g, rows_hi, rows_lo):
    one, zero = jnp.ones((), jnp.bfloat16), jnp.zeros((), jnp.bfloat16)
    h = jnp.broadcast_to(hi_s[pl.ds(g, 1), :], (16, 256)).astype(jnp.bfloat16)
    l = jnp.broadcast_to(lo_s[pl.ds(g, 1), :], (16, 256)).astype(jnp.bfloat16)
    left = jnp.where(rows_hi == h[None], one, zero).reshape(128, 256)
    right = jnp.where(rows_lo == l[None], one, zero).reshape(256, 256)
    return lax.dot_general(left, right, NT, preferred_element_type=jnp.float32)


def aggregate_block(b, src_s, hi_s, lo_s, tal, agg_s):
    def rows(n):
        ids = lax.broadcasted_iota(jnp.int32, (n, 256), 0).astype(jnp.float32)
        return ids.astype(jnp.bfloat16).reshape(n // 16, 16, 256)

    rows_hi, rows_lo = rows(128), rows(256)

    def pair(p, _):
        g = b * 32 + p * 2
        first = tally(hi_s, lo_s, g, rows_hi, rows_lo).reshape(16, 1, 8, 256)
        second = tally(hi_s, lo_s, g + 1, rows_hi, rows_lo).reshape(16, 1, 8, 256)
        both = jnp.concatenate([first, second], axis=1).reshape(16, 16, 256)
        tal[:, pl.ds(pl.multiple_of(p * 16, 16), 16), :] = both.astype(jnp.bfloat16)
        return 0

    lax.fori_loop(0, 16, pair, 0, unroll=8)
    total = jnp.zeros((256, F), jnp.float32)
    for h in range(16):
        total += lax.dot_general(tal[h], src_s[:, h * 256 : (h + 1) * 256], NT, preferred_element_type=jnp.float32)
    agg_s[pl.ds(pl.multiple_of(b * 256, 256), 256), 0:F] = total


def kernel(
    src_hbm, nbr_hbm, deg_hbm, counts_ref, up_hbm, pre_hbm,
    self_ref, neigh_ref, bias_ref,
    src_s, nbr_s, deg_s, up_s, pre_s, hi_s, lo_s, tal, agg_s, lhs, dz, part, rs, mine, ag,
    load_sem, up_send, up_recv, dn_send, dn_recv, sib_send, sib_recv, rs_send, rs_recv, ag_send, ag_recv,
):
    dp, col = lax.axis_index("dp"), lax.axis_index("col")
    y, x, z, core = dp // NX, dp % NX, col // 2, col % 2
    above, below = (z + 1) % NZ * 2 + core, (z + NZ - 1) % NZ * 2 + core
    sibling = z * 2 + 1 - core

    def peer(d):
        return (y + d // NX) % NY * NX + (x + d % NX) % NX

    barrier = pltpu.get_barrier_semaphore()
    for near in (above, below, sibling):
        pl.semaphore_signal(barrier, inc=1, device_id=(dp, near), device_id_type=MESH)

    loads = [
        pltpu.make_async_copy(a, b, load_sem.at[i])
        for i, (a, b) in enumerate(
            ((up_hbm, up_s), (pre_hbm, pre_s), (nbr_hbm, nbr_s), (deg_hbm, deg_s), (src_hbm, src_s))
        )
    ]
    for load in loads:
        load.start()

    def greet(d, _):
        pl.semaphore_signal(barrier, inc=1, device_id=(peer(d), col), device_id_type=MESH)
        return 0

    lax.fori_loop(1, NDP, greet, 0)

    loads[0].wait()
    loads[1].wait()
    limit = counts_ref[0]
    row = col * ROWS + lax.broadcasted_iota(jnp.int32, (ROWS, W), 0)
    for q in range(C):
        at = slice(q * W, (q + 1) * W)
        keep = (pre_s[:, at].astype(jnp.float32) > 0) & (row < limit)
        dz[q, col] = jnp.where(keep, up_s[:, at].astype(jnp.float32), 0.0).astype(jnp.bfloat16)

    pl.semaphore_wait(barrier, 3 + NP)

    def send(ref, send_sem, recv_sem, to):
        return pltpu.make_async_remote_copy(
            src_ref=ref, dst_ref=ref, send_sem=send_sem, recv_sem=recv_sem, device_id=to, device_id_type=MESH
        )

    def up(q, s, slot, rows):
        return send(dz.at[q, slot, rows], up_send.at[q, s], up_recv.at[q, s], (dp, above))

    def dn(q, s, slot, rows):
        return send(dz.at[q, slot, rows], dn_send.at[q, s], dn_recv.at[q, s], (dp, below))

    def sib(q, i, slot):
        return send(dz.at[q, slot], sib_send.at[q, i], sib_recv.at[q, i], (dp, sibling))

    whole, low, high = pl.ds(0, ROWS), pl.ds(0, ROWS // 2), pl.ds(ROWS // 2, ROWS // 2)
    for q in range(C):
        up(q, 0, col, whole).start()
        dn(q, 0, col, whole).start()
        sib(q, 0, col).start()

    def serve(s, q):
        from_below = (z + NZ - s) % NZ * 2 + core
        from_above = (z + s) % NZ * 2 + core

        @pl.when(s < 4)
        def _():
            up(q, s - 1, from_below, whole).wait_recv()

            @pl.when(s < 3)
            def _():
                up(q, s, from_below, whole).start()

            @pl.when(s == 3)
            def _():
                up(q, s, from_below, low).start()

            dn(q, s - 1, from_above, whole).wait_recv()

            @pl.when(s < 3)
            def _():
                dn(q, s, from_above, whole).start()

            @pl.when(s == 3)
            def _():
                dn(q, s, from_above, high).start()

            sib(q, s, from_below).start()
            sib(q, 3 + s, from_above).start()

        @pl.when(s == 4)
        def _():
            up(q, s - 1, from_below, low).wait_recv()
            dn(q, s - 1, from_below, high).wait_recv()
            sib(q, 7, from_below).start()

    loads[2].wait()
    loads[3].wait()
    encode(nbr_s, deg_s, hi_s, lo_s)
    loads[4].wait()

    def step(i, _):
        aggregate_block(i, src_s, hi_s, lo_s, tal, agg_s)
        serve(1 + i // C, i % C)
        return 0

    lax.fori_loop(0, 8, step, 0)

    lhs[0:F] = src_s[:, 0:T]
    for j in range(8):
        at = slice(j * 256, (j + 1) * 256)
        total = agg_s[pl.ds(j, 256, stride=8), :].T
        lhs[F : 2 * F, at] = (total[0:F] / jnp.maximum(deg_s[:, at], 1).astype(jnp.float32)).astype(jnp.bfloat16)
    lhs[2 * F : 2 * F + 16] = jnp.ones((16, T), jnp.bfloat16)

    scale = jnp.float32(1.0) / jnp.sqrt(jnp.float32(T * NDP))
    for q in range(C):
        for i in range(8):
            slot = lax.rem(z + NZ, NZ) * 2 + core
            sib(q, i, slot).wait_recv()
        grad = jnp.dot(lhs[...], dz[q].reshape(T, W), preferred_element_type=jnp.float32)
        for b in range(W // 128):
            at = slice(b * 128, (b + 1) * 128)
            for a in range(4):
                part[a * 8 + q * (W // 128) + b, 0:24] = grad[a * 24 : a * 24 + 24, at]
                part[a * 8 + q * (W // 128) + b, 24:32] = grad[96:104, at]

    def rs_copy(d):
        return pltpu.make_async_remote_copy(
            src_ref=part.at[peer(d)], dst_ref=rs.at[d], send_sem=rs_send, recv_sem=rs_recv,
            device_id=(peer(d), col), device_id_type=MESH,
        )

    def rs_start(d, _):
        rs_copy(d).start()
        return 0

    lax.fori_loop(1, NDP, rs_start, 0)
    rs[0] = part[dp]
    pltpu.make_async_copy(rs.at[pl.ds(1, NP)], rs.at[pl.ds(1, NP)], rs_recv).wait()

    total = rs[0]
    for d in range(1, NDP):
        total += rs[d]
    mine[...] = total * scale
    ag[dp] = mine[...]

    def ag_start(d, _):
        pltpu.make_async_remote_copy(
            src_ref=mine, dst_ref=ag.at[dp], send_sem=ag_send, recv_sem=ag_recv,
            device_id=(peer(d), col), device_id_type=MESH,
        ).start()
        return 0

    lax.fori_loop(1, NDP, ag_start, 0)
    pltpu.make_async_copy(ag.at[pl.ds(1, NP)], ag.at[pl.ds(1, NP)], ag_recv).wait()
    for b in range(8):
        at = slice(b * 128, (b + 1) * 128)
        for a in range(2):
            self_ref[a * 24 : a * 24 + 24, at] = ag[a * 8 + b, 0:24]
            neigh_ref[a * 24 : a * 24 + 24, at] = ag[(a + 2) * 8 + b, 0:24]
        bias_ref[:, at] = ag[b, 24:25]

    for q in range(C):
        for s in range(4):
            up(q, s, col, whole if s < 3 else low).wait_send()
            dn(q, s, col, whole if s < 3 else high).wait_send()
        for i in range(8):
            sib(q, i, col).wait_send()
    pltpu.make_async_copy(part.at[pl.ds(1, NP)], part.at[pl.ds(1, NP)], rs_send).wait()
    pltpu.make_async_copy(ag.at[pl.ds(1, NP)], ag.at[pl.ds(1, NP)], ag_send).wait()


def per_device(source_feats, neighbours, degree, counts, upstream, preact):
    any_, vmem = pl.BlockSpec(memory_space=pl.ANY), pl.BlockSpec(memory_space=pltpu.VMEM)
    dma = pltpu.SemaphoreType.DMA
    f32, bf16, i32 = jnp.float32, jnp.bfloat16, jnp.int32
    grad = jax.ShapeDtypeStruct((F, H), f32)
    out = pl.pallas_call(
        kernel,
        out_shape=(grad, grad, jax.ShapeDtypeStruct((1, H), f32)),
        in_specs=[any_, any_, any_, pl.BlockSpec(memory_space=pltpu.SMEM), any_, any_],
        out_specs=(vmem, vmem, vmem),
        scratch_shapes=[
            pltpu.VMEM((F, 4096), bf16),
            pltpu.VMEM((25, T), i32),
            pltpu.VMEM((1, T), i32),
            pltpu.VMEM((ROWS, H), bf16),
            pltpu.VMEM((ROWS, H), bf16),
            pltpu.VMEM((256, 256), f32),
            pltpu.VMEM((256, 256), f32),
            pltpu.VMEM((16, 256, 256), bf16),
            pltpu.VMEM((T, 128), f32),
            pltpu.VMEM((2 * F + 16, T), bf16),
            pltpu.VMEM((C, NCOL, ROWS, W), bf16),
            pltpu.VMEM((NDP, 32, 128), f32),
            pltpu.VMEM((NDP, 32, 128), f32),
            pltpu.VMEM((32, 128), f32),
            pltpu.VMEM((NDP, 32, 128), f32),
            dma((5,)),
            dma((C, 4)), dma((C, 4)), dma((C, 4)), dma((C, 4)), dma((C, 8)), dma((C, 8)),
            dma(()), dma(()), dma(()), dma(()),
        ],
        compiler_params=pltpu.CompilerParams(collective_id=0, has_side_effects=True, vmem_limit_bytes=40 << 20),
        name="sage_grads",
    )(source_feats, neighbours.T, degree.reshape(1, T), counts, upstream, preact)
    return out[0], out[1], out[2].reshape(H)


def solution(mesh):
    placed = (P("col", "dp"), P("dp", None), P("dp"), P("dp"), P(("dp", "col"), None), P(("dp", "col"), None))
    return jax.shard_map(
        per_device,
        mesh=mesh,
        in_specs=placed,
        out_specs=(P("col", None), P("col", None), P()),
        check_vma=False,
    )
```

time: 527 us -> 81.6 us (0.15)
  other arithmetic: 332 us -> 0 us
  blocking collectives: 108 us -> 0 us
  Pallas kernels: 0 us -> 73.3 us
  waiting for transfers between devices: 49.4 us -> 0 us
  matrix products: 17.5 us -> 0 us
  between operations: 14.7 us -> 1.3 us
    reduce_sum x5 -> x0, other arithmetic: 330 us -> none  [the longest x4 328 us: one_block(): tally = jnp.sum(hits.astype(jnp.float32), axis=2).astype(jnp.bfloat16)]
    psum x1 -> x0, blocking collectives: 108 us -> none  [per_device(): summed_bias = lax.psum(local_bias, ('dp', 'col'))]
    pallas_call x0 -> x1, Pallas kernels: none -> 73.3 us  [per_device(): pl.pallas_call(kernel, out_shape=(grad, grad, jax.ShapeDtypeStruct((1, H)...]
    psum x1 -> x0, waiting for transfers between devices: 49.3 us -> none  [per_device(): lax.psum((jnp.dot(self_feats, piece, preferred_element_type=jnp.float32),...]
    dot_general x6 -> x0, matrix products: 17.5 us -> none  [the longest x4 12 us: one_block(): total = jnp.dot(source_cols, tally, preferred_element_type=jnp.float32)]
    unnamed x2 -> x13, local copies, waits for them, and re-layouts: 0.01 us -> 6.48 us
  transfers between devices with their start and end apart: 2 -> 0, of which waited for: 1 -> 0; matrix products, arithmetic and copies ran while one was open for 65% -> 0% of each run, Pallas kernels for 0% -> 0%
where the time goes in v1:
time: 81.6 us; the launch traced here: 81.1 us
  Pallas kernels  73.3 us (90%)
  local copies, waits for them, and re-layouts  6.48 us (8%)
  between operations  1.3 us (2%)
    pallas_call x1, Pallas kernels, per_device(): pl.pallas_call(kernel, out_shape=(grad, grad, jax.ShapeDtypeStruct((1, H)...  73.3 us
    unnamed x13, local copies, waits for them, and re-layouts  6.48 us

profile of v1, /device:TPU:1, one launch (start us, length us, event | category | flops | bytes accessed | tf_op | source)
XLA Modules:
  0.0 81.1 jit_solution(4479854516268598346)
XLA Ops:
  1.3 0.0 copy-start
  1.3 1.0 %copy-done = bf16[48,4096]{1,0:T(8,128)(2,1)S(1)} copy-done((bf16[48,4096]{1,0:T(8,128)(2,1)S(1)}, bf16[48,4096]{1,0:T(8,128)(2,1)}, u32[]{:S(2)}) %copy-start) | copy-done | bytes 393240
  2.3 0.0 copy-start.1
  2.3 0.9 %copy-done.1 = s32[2048,25]{0,1:T(8,128)S(1)} copy-done((s32[2048,25]{0,1:T(8,128)S(1)}, s32[2048,25]{0,1:T(8,128)}, u32[]{:S(2)}) %copy-start.1) | copy-done | bytes 204824
  3.2 0.0 copy-start.2
  3.2 0.9 %copy-done.2 = bf16[128,1024]{1,0:T(8,128)(2,1)S(1)} copy-done((bf16[128,1024]{1,0:T(8,128)(2,1)S(1)}, bf16[128,1024]{1,0:T(8,128)(2,1)}, u32[]{:S(2)}) %copy-start.2) | copy-done | bytes 262168
  4.2 0.0 copy-start.3
  4.2 0.9 %copy-done.3 = bf16[128,1024]{1,0:T(8,128)(2,1)S(1)} copy-done((bf16[128,1024]{1,0:T(8,128)(2,1)S(1)}, bf16[128,1024]{1,0:T(8,128)(2,1)}, u32[]{:S(2)}) %copy-start.3) | copy-done | bytes 262168
  5.1 0.0 copy-start.4
  5.1 0.7 copy-done.4
  5.8 73.3 %sage_grads.1 = (f32[48,1024]{1,0:T(8,128)S(1)}, f32[48,1024]{1,0:T(8,128)S(1)}, f32[1,1024]{1,0:T(1,128)S(1)}) custom-call(bf16[48,4096]{1,0:T(8,128)(2,1)S(1)} %copy-done, s32[25,2048]{1,0:T(8,128)S(1)} %bitcast.3, s32[1,2048]{1,0:T(1,128)S(1)} %bitcast.4, s32[1]{0:T(128)S(6)} %copy.12.counts_ref, bf16[128,1024]{1,0:T(8,128)(2,1)S(1)} %copy-done.2, ...), custom_call_target="tpu_custom_call" | custom-call | tf_op jit(solution)/shard_map/sage_grads/pallas_call | solution.py:246
  79.1 0.7 copy.13
  79.8 0.7 copy.14
  80.5 0.6 copy.15
Async XLA Ops:
  1.3 1.0 %copy-start = (bf16[48,4096]{1,0:T(8,128)(2,1)S(1)}, bf16[48,4096]{1,0:T(8,128)(2,1)}, u32[]{:S(2)}) copy-start(bf16[48,4096]{1,0:T(8,128)(2,1)} %src_hbm.1) | copy-start | bytes 1179652
  2.3 0.9 %copy-start.1 = (s32[2048,25]{0,1:T(8,128)S(1)}, s32[2048,25]{0,1:T(8,128)}, u32[]{:S(2)}) copy-start(s32[2048,25]{0,1:T(8,128)} %param.7) | copy-start | bytes 614404
  3.2 0.9 %copy-start.2 = (bf16[128,1024]{1,0:T(8,128)(2,1)S(1)}, bf16[128,1024]{1,0:T(8,128)(2,1)}, u32[]{:S(2)}) copy-start(bf16[128,1024]{1,0:T(8,128)(2,1)} %up_hbm.1) | copy-start | bytes 786436
  4.2 0.9 %copy-start.3 = (bf16[128,1024]{1,0:T(8,128)(2,1)S(1)}, bf16[128,1024]{1,0:T(8,128)(2,1)}, u32[]{:S(2)}) copy-start(bf16[128,1024]{1,0:T(8,128)(2,1)} %pre_hbm.1) | copy-start | bytes 786436
  5.1 0.7 copy-start.4

commit v2 on v1

v2 whole, which is shorter than its diff:
```python
import jax
import jax.numpy as jnp
from jax import lax
from jax.experimental import pallas as pl
from jax.experimental.pallas import tpu as pltpu
from jax.sharding import PartitionSpec as P

MESH = pl.DeviceIdType.MESH
NT = (((1,), (1,)), ((), ()))
NZ, NY, NX = 8, 8, 4
NDP, NCOL = NY * NX, NZ * 2
C = 2
H = 1024
W = H // C
ROWS = 128
T = 2048
F = 48
NP = NDP - 1
ONEHOT = jnp.float8_e4m3fn
PEERS = sorted(
    ((dy, dx) for dy in range(NY) for dx in range(NX) if dy or dx),
    key=lambda p: -(min(p[0], NY - p[0]) + min(p[1], NX - p[1])),
)


def encode(nbr_ref, deg_ref, hi_s, lo_s):
    k, t = nbr_ref.shape
    nb = nbr_ref[...]
    live = lax.broadcasted_iota(jnp.int32, (k, t), 0) < deg_ref[...]
    j = lax.broadcasted_iota(jnp.int32, (k, t), 1) // 256
    hi = jnp.where(live, (nb >> 8) * 8 + j, 255).astype(jnp.float32)
    lo = (nb & 255).astype(jnp.float32)
    pad = jnp.full((32 - k, t), 255.0, jnp.float32)
    for code, out in ((hi, hi_s), (lo, lo_s)):
        code = jnp.concatenate([code, pad], axis=0)
        out[...] = jnp.concatenate([code[:, i * 256 : (i + 1) * 256] for i in range(8)], axis=0).T


def tally(hi_s, lo_s, g, rows_hi, rows_lo):
    one, zero = jnp.ones((), jnp.bfloat16), jnp.zeros((), jnp.bfloat16)
    h = jnp.broadcast_to(hi_s[pl.ds(g, 1), :], (16, 256)).astype(jnp.bfloat16)
    l = jnp.broadcast_to(lo_s[pl.ds(g, 1), :], (16, 256)).astype(jnp.bfloat16)
    left = jnp.where(rows_hi == h[None], one, zero).reshape(128, 256).astype(ONEHOT)
    right = jnp.where(rows_lo == l[None], one, zero).reshape(256, 256).astype(ONEHOT)
    return lax.dot_general(left, right, NT, preferred_element_type=jnp.float32)


def aggregate_block(b, src_s, hi_s, lo_s, tal, agg_s):
    def rows(n):
        ids = lax.broadcasted_iota(jnp.int32, (n, 256), 0).astype(jnp.float32)
        return ids.astype(jnp.bfloat16).reshape(n // 16, 16, 256)

    rows_hi, rows_lo = rows(128), rows(256)

    def pair(p, _):
        g = b * 32 + p * 2
        first = tally(hi_s, lo_s, g, rows_hi, rows_lo).reshape(16, 1, 8, 256)
        second = tally(hi_s, lo_s, g + 1, rows_hi, rows_lo).reshape(16, 1, 8, 256)
        both = jnp.concatenate([first, second], axis=1).reshape(16, 16, 256)
        tal[:, pl.ds(pl.multiple_of(p * 16, 16), 16), :] = both.astype(jnp.bfloat16)
        return 0

    lax.fori_loop(0, 16, pair, 0, unroll=16)
    total = jnp.zeros((256, F), jnp.float32)
    for h in range(16):
        total += lax.dot_general(tal[h], src_s[:, h * 256 : (h + 1) * 256], NT, preferred_element_type=jnp.float32)
    agg_s[pl.ds(pl.multiple_of(b * 256, 256), 256), 0:F] = total


def kernel(
    src_hbm, nbr_hbm, deg_hbm, counts_ref, up_hbm, pre_hbm,
    grad_ref, bias_ref,
    src_s, nbr_s, deg_s, up_s, pre_s, hi_s, lo_s, tal, agg_s, lhs, dz, acc, part, rs, mine,
    load_sem, up_send, up_recv, dn_send, dn_recv, sib_send, sib_recv, rs_send, rs_recv, ag_send, ag_recv, own_sem,
):
    dp, col = lax.axis_index("dp"), lax.axis_index("col")
    y, x, z, core = dp // NX, dp % NX, col // 2, col % 2
    above, below = (z + 1) % NZ * 2 + core, (z + NZ - 1) % NZ * 2 + core
    sibling = z * 2 + 1 - core

    def peer(dy, dx):
        return (y + dy) % NY * NX + (x + dx) % NX

    barrier = pltpu.get_barrier_semaphore()
    for near in (above, below, sibling):
        pl.semaphore_signal(barrier, inc=1, device_id=(dp, near), device_id_type=MESH)

    loads = [
        pltpu.make_async_copy(a, b, load_sem.at[i])
        for i, (a, b) in enumerate(
            ((up_hbm, up_s), (pre_hbm, pre_s), (nbr_hbm, nbr_s), (deg_hbm, deg_s), (src_hbm, src_s))
        )
    ]
    for load in loads:
        load.start()

    for p in PEERS:
        pl.semaphore_signal(barrier, inc=1, device_id=(peer(*p), col), device_id_type=MESH)

    loads[0].wait()
    loads[1].wait()
    limit = counts_ref[0]
    row = col * ROWS + lax.broadcasted_iota(jnp.int32, (ROWS, W), 0)
    for q in range(C):
        at = slice(q * W, (q + 1) * W)
        keep = (pre_s[:, at].astype(jnp.float32) > 0) & (row < limit)
        dz[q, col] = jnp.where(keep, up_s[:, at].astype(jnp.float32), 0.0).astype(jnp.bfloat16)

    pl.semaphore_wait(barrier, 3 + NP)

    def send(ref, send_sem, recv_sem, to):
        return pltpu.make_async_remote_copy(
            src_ref=ref, dst_ref=ref, send_sem=send_sem, recv_sem=recv_sem, device_id=to, device_id_type=MESH
        )

    def up(q, s, slot, rows):
        return send(dz.at[q, slot, rows], up_send.at[q, s], up_recv.at[q, s], (dp, above))

    def dn(q, s, slot, rows):
        return send(dz.at[q, slot, rows], dn_send.at[q, s], dn_recv.at[q, s], (dp, below))

    def sib(q, i, slot):
        return send(dz.at[q, slot], sib_send.at[q, i], sib_recv.at[q, i], (dp, sibling))

    whole, low, high = pl.ds(0, ROWS), pl.ds(0, ROWS // 2), pl.ds(ROWS // 2, ROWS // 2)
    for q in range(C):
        up(q, 0, col, whole).start()
        dn(q, 0, col, whole).start()
        sib(q, 0, col).start()

    def serve(s, q):
        from_below = (z + NZ - s) % NZ * 2 + core
        from_above = (z + s) % NZ * 2 + core
        if s == 4:
            up(q, s - 1, from_below, low).wait_recv()
            dn(q, s - 1, from_below, high).wait_recv()
            sib(q, 7, from_below).start()
            return
        up(q, s - 1, from_below, whole).wait_recv()
        up(q, s, from_below, whole if s < 3 else low).start()
        dn(q, s - 1, from_above, whole).wait_recv()
        dn(q, s, from_above, whole if s < 3 else high).start()
        sib(q, s, from_below).start()
        sib(q, 3 + s, from_above).start()

    def add(dz_, i):
        at = (z + NZ + dz_) % NZ
        for q in range(C):
            sib(q, i, at * 2 + 1 - core).wait_recv()
        rows = lhs[:, pl.ds(pl.multiple_of(at * 2 * ROWS, 2 * ROWS), 2 * ROWS)]
        for q in range(C):
            new = jnp.dot(rows, dz[q, pl.ds(at * 2, 2)].reshape(2 * ROWS, W), preferred_element_type=jnp.float32)
            here = slice(q * W, (q + 1) * W)
            acc[:, here] = new if dz_ == 0 else acc[:, here] + new

    loads[2].wait()
    loads[3].wait()
    encode(nbr_s, deg_s, hi_s, lo_s)
    loads[4].wait()

    def step(i, _):
        aggregate_block(i, src_s, hi_s, lo_s, tal, agg_s)
        for at, turn in ((3, (1, 0)), (4, (1, 1)), (7, (2, 0))):
            pl.when(i == at)(lambda turn=turn: serve(*turn))
        return 0

    lax.fori_loop(0, 8, step, 0)

    lhs[0:F] = src_s[:, 0:T]
    for j in range(8):
        at = slice(j * 256, (j + 1) * 256)
        total = agg_s[pl.ds(j, 256, stride=8), :].T
        lhs[F : 2 * F, at] = (total[0:F] / jnp.maximum(deg_s[:, at], 1).astype(jnp.float32)).astype(jnp.bfloat16)
    lhs[2 * F : 2 * F + 16] = jnp.ones((16, T), jnp.bfloat16)

    serve(2, 1)
    add(0, 0)
    add(-1, 1)
    add(1, 4)
    serve(3, 0)
    serve(3, 1)
    add(-2, 2)
    add(2, 5)
    serve(4, 0)
    serve(4, 1)
    add(-3, 3)
    add(3, 6)
    add(4, 7)

    bias = jnp.concatenate([acc[2 * F : 2 * F + 1, b * 128 : (b + 1) * 128] for b in range(8)], axis=0)
    for a in range(4):
        for b in range(8):
            rows = acc[a * 24 : a * 24 + 24, b * 128 : (b + 1) * 128]
            part[a * 8 + b] = jnp.concatenate([rows, bias], axis=0).astype(jnp.bfloat16)

    for p in PEERS:
        pltpu.make_async_remote_copy(
            src_ref=part.at[peer(*p)], dst_ref=rs.at[dp], send_sem=rs_send, recv_sem=rs_recv,
            device_id=(peer(*p), col), device_id_type=MESH,
        ).start()
    rs[dp] = part[dp]
    pltpu.make_async_copy(rs.at[pl.ds(0, NP)], rs.at[pl.ds(0, NP)], rs_recv).wait()

    scale = jnp.float32(1.0) / jnp.sqrt(jnp.float32(T * NDP))
    total = rs[0].astype(jnp.float32)
    for d in range(1, NDP):
        total += rs[d].astype(jnp.float32)
    total *= scale
    mine[...] = total[0:24]
    bias_ref[...] = total[24:32]

    rows, cols = pl.ds(pl.multiple_of(dp // 8 * 24, 8), 24), pl.ds(pl.multiple_of(dp % 8 * 128, 128), 128)
    for p in PEERS:
        pltpu.make_async_remote_copy(
            src_ref=mine, dst_ref=grad_ref.at[rows, cols], send_sem=ag_send, recv_sem=ag_recv,
            device_id=(peer(*p), col), device_id_type=MESH,
        ).start()
    own = pltpu.make_async_copy(mine, grad_ref.at[rows, cols], own_sem)
    own.start()

    for q in range(C):
        for s in range(4):
            up(q, s, col, whole if s < 3 else low).wait_send()
            dn(q, s, col, whole if s < 3 else high).wait_send()
        for i in range(8):
            sib(q, i, col).wait_send()
    pltpu.make_async_copy(part.at[pl.ds(0, NP)], part.at[pl.ds(0, NP)], rs_send).wait()
    own.wait()
    every = agg_s.at[pl.ds(0, NP * 24)]
    pltpu.make_async_copy(every, every, ag_send).wait()
    pltpu.make_async_copy(every, every, ag_recv).wait()


def place(grad_ref, bias_ref, self_ref, neigh_ref, out_ref, sems):
    copies = (
        pltpu.make_async_copy(grad_ref.at[pl.ds(0, F)], self_ref, sems.at[0]),
        pltpu.make_async_copy(grad_ref.at[pl.ds(F, F)], neigh_ref, sems.at[1]),
        pltpu.make_async_copy(bias_ref, out_ref, sems.at[2]),
    )
    for copy in copies:
        copy.start()
    for copy in copies:
        copy.wait()


def per_device(source_feats, neighbours, degree, counts, upstream, preact):
    any_, vmem = pl.BlockSpec(memory_space=pl.ANY), pl.BlockSpec(memory_space=pltpu.VMEM)
    dma = pltpu.SemaphoreType.DMA
    f32, bf16, i32 = jnp.float32, jnp.bfloat16, jnp.int32
    grad, bias = pl.pallas_call(
        kernel,
        out_shape=(jax.ShapeDtypeStruct((2 * F, H), f32), jax.ShapeDtypeStruct((8, 128), f32)),
        in_specs=[any_, any_, any_, pl.BlockSpec(memory_space=pltpu.SMEM), any_, any_],
        out_specs=(any_, vmem),
        scratch_shapes=[
            pltpu.VMEM((F, 4096), bf16),
            pltpu.VMEM((25, T), i32),
            pltpu.VMEM((1, T), i32),
            pltpu.VMEM((ROWS, H), bf16),
            pltpu.VMEM((ROWS, H), bf16),
            pltpu.VMEM((256, 256), f32),
            pltpu.VMEM((256, 256), f32),
            pltpu.VMEM((16, 256, 256), bf16),
            pltpu.VMEM((T, 128), f32),
            pltpu.VMEM((2 * F + 16, T), bf16),
            pltpu.VMEM((C, NCOL, ROWS, W), bf16),
            pltpu.VMEM((2 * F + 16, H), f32),
            pltpu.VMEM((NDP, 32, 128), bf16),
            pltpu.VMEM((NDP, 32, 128), bf16),
            pltpu.VMEM((24, 128), f32),
            dma((5,)),
            dma((C, 4)), dma((C, 4)), dma((C, 4)), dma((C, 4)), dma((C, 8)), dma((C, 8)),
            dma(()), dma(()), dma(()), dma(()), dma(()),
        ],
        compiler_params=pltpu.CompilerParams(collective_id=0, has_side_effects=True, vmem_limit_bytes=60 << 20),
        name="sage_grads",
    )(source_feats, neighbours.T, degree.reshape(1, T), counts, upstream, preact)
    own, neigh, bias = pl.pallas_call(
        place,
        out_shape=(jax.ShapeDtypeStruct((F, H), f32), jax.ShapeDtypeStruct((F, H), f32), jax.ShapeDtypeStruct((8, 128), f32)),
        in_specs=[any_, any_],
        out_specs=(any_, any_, any_),
        scratch_shapes=[dma((3,))],
        compiler_params=pltpu.CompilerParams(vmem_limit_bytes=60 << 20),
        name="place",
    )(grad, bias)
    return own, neigh, bias.reshape(H)


def solution(mesh):
    placed = (P("col", "dp"), P("dp", None), P("dp"), P("dp"), P(("dp", "col"), None), P(("dp", "col"), None))
    return jax.shard_map(
        per_device,
        mesh=mesh,
        in_specs=placed,
        out_specs=(P("col", None), P("col", None), P()),
        check_vma=False,
    )
```

time: 81.6 us -> 76.9 us (0.942)
  local copies, waits for them, and re-layouts: 6.48 us -> 0 us
  Pallas kernels: 73.3 us -> 75.5 us
    unnamed x13 -> x0, local copies, waits for them, and re-layouts: 6.48 us -> none
    pallas_call x1 -> x2, Pallas kernels: 73.3 us -> 75.5 us  [the longest x1 62.3 us: per_device(): pl.pallas_call(kernel, out_shape=(jax.ShapeDtypeStruct((2 * F, H), f32),...]
where the time goes in v2:
time: 76.9 us; the launch traced here: 76.8 us
  Pallas kernels  75.5 us (98%)
  between operations  1.29 us (2%)
    pallas_call x1, Pallas kernels, per_device(): pl.pallas_call(kernel, out_shape=(jax.ShapeDtypeStruct((2 * F, H), f32),...  62.3 us
    pallas_call x1, Pallas kernels, per_device(): pl.pallas_call(place, out_shape=(jax.ShapeDtypeStruct((F, H), f32), jax.S...  13.2 us

profile of v2, /device:TPU:1, one launch (start us, length us, event | category | flops | bytes accessed | tf_op | source)
XLA Modules:
  0.0 76.8 jit_solution(5024307550862599164)
XLA Ops:
  1.3 62.3 %sage_grads.1 = (f32[96,1024]{1,0:T(8,128)}, f32[8,128]{1,0:T(8,128)}) custom-call(bf16[48,4096]{1,0:T(8,128)(2,1)} %src_hbm.1, s32[25,2048]{1,0:T(8,128)} %bitcast.3, s32[1,2048]{1,0:T(1,128)} %bitcast.4, s32[1]{0:T(128)S(6)} %copy.9.counts_ref, bf16[128,1024]{1,0:T(8,128)(2,1)} %up_hbm.1, bf16[128,1024]{1,0:T(8,128)(2,1)} %pre_hbm.1), custom_call_target="tpu_custom_call" | custom-call | tf_op jit(solution)/shard_map/sage_grads/pallas_call | solution.py:250
  63.6 13.2 %place.1 = (f32[48,1024]{1,0:T(8,128)}, f32[48,1024]{1,0:T(8,128)}, f32[8,128]{1,0:T(8,128)}) custom-call(f32[96,1024]{1,0:T(8,128)} %get-tuple-element.8.grad_ref, f32[8,128]{1,0:T(8,128)} %get-tuple-element.9.bias_ref), custom_call_target="tpu_custom_call" | custom-call | tf_op jit(solution)/shard_map/place/pallas_call | solution.py:278

commit v3 on v2

--- a/solution.py
+++ b/solution.py
@@ -71,7 +71,7 @@
     src_hbm, nbr_hbm, deg_hbm, counts_ref, up_hbm, pre_hbm,
     grad_ref, bias_ref,
     src_s, nbr_s, deg_s, up_s, pre_s, hi_s, lo_s, tal, agg_s, lhs, dz, acc, part, rs, mine,
-    load_sem, up_send, up_recv, dn_send, dn_recv, sib_send, sib_recv, rs_send, rs_recv, ag_send, ag_recv, own_sem,
+    load_sem, up_send, up_recv, dn_send, dn_recv, sib_send, sib_recv, rs_send, rs_recv, ag_send, ag_recv, own_sem, news,
 ):
     dp, col = lax.axis_index("dp"), lax.axis_index("col")
     y, x, z, core = dp // NX, dp % NX, col // 2, col % 2
@@ -82,8 +82,10 @@
         return (y + dy) % NY * NX + (x + dx) % NX
 
     barrier = pltpu.get_barrier_semaphore()
-    for near in (above, below, sibling):
-        pl.semaphore_signal(barrier, inc=1, device_id=(dp, near), device_id_type=MESH)
+    beside_x, beside_y = (peer(0, 1), peer(0, NX - 1)), (peer(1, 0), peer(NY - 1, 0))
+    near = [(dp, above), (dp, below), (dp, sibling)] + [(p, col) for p in beside_x + beside_y]
+    for to in near:
+        pl.semaphore_signal(barrier, inc=1, device_id=to, device_id_type=MESH)
 
     loads = [
         pltpu.make_async_copy(a, b, load_sem.at[i])
@@ -94,8 +96,6 @@
     for load in loads:
         load.start()
 
-    for p in PEERS:
-        pl.semaphore_signal(barrier, inc=1, device_id=(peer(*p), col), device_id_type=MESH)
 
     loads[0].wait()
     loads[1].wait()
@@ -106,7 +106,18 @@
         keep = (pre_s[:, at].astype(jnp.float32) > 0) & (row < limit)
         dz[q, col] = jnp.where(keep, up_s[:, at].astype(jnp.float32), 0.0).astype(jnp.bfloat16)
 
-    pl.semaphore_wait(barrier, 3 + NP)
+    pl.semaphore_wait(barrier, len(near))
+
+    def tell(n):
+        for to in beside_x if n == 0 else beside_y:
+            pl.semaphore_signal(news.at[n], inc=1, device_id=(to, col), device_id_type=MESH)
+
+    def hear(n):
+        pl.semaphore_wait(news.at[n], 2)
+        if n < NY // 2:
+            tell(n + 1)
+
+    tell(0)
 
     def send(ref, send_sem, recv_sem, to):
         return pltpu.make_async_remote_copy(
@@ -160,6 +171,8 @@
 
     def step(i, _):
         aggregate_block(i, src_s, hi_s, lo_s, tal, agg_s)
+        for at, n in ((1, 0), (4, 1), (6, 2)):
+            pl.when(i == at)(lambda n=n: hear(n))
         for at, turn in ((3, (1, 0)), (4, (1, 1)), (7, (2, 0))):
             pl.when(i == at)(lambda turn=turn: serve(*turn))
         return 0
@@ -174,6 +187,7 @@
     lhs[2 * F : 2 * F + 16] = jnp.ones((16, T), jnp.bfloat16)
 
     serve(2, 1)
+    hear(3)
     add(0, 0)
     add(-1, 1)
     add(1, 4)
@@ -193,6 +207,7 @@
             rows = acc[a * 24 : a * 24 + 24, b * 128 : (b + 1) * 128]
             part[a * 8 + b] = jnp.concatenate([rows, bias], axis=0).astype(jnp.bfloat16)
 
+    hear(4)
     for p in PEERS:
         pltpu.make_async_remote_copy(
             src_ref=part.at[peer(*p)], dst_ref=rs.at[dp], send_sem=rs_send, recv_sem=rs_recv,
@@ -231,16 +246,10 @@
     pltpu.make_async_copy(every, every, ag_recv).wait()
 
 
-def place(grad_ref, bias_ref, self_ref, neigh_ref, out_ref, sems):
-    copies = (
-        pltpu.make_async_copy(grad_ref.at[pl.ds(0, F)], self_ref, sems.at[0]),
-        pltpu.make_async_copy(grad_ref.at[pl.ds(F, F)], neigh_ref, sems.at[1]),
-        pltpu.make_async_copy(bias_ref, out_ref, sems.at[2]),
-    )
-    for copy in copies:
-        copy.start()
-    for copy in copies:
-        copy.wait()
+def place(grad_ref, bias_ref, self_ref, neigh_ref, out_ref):
+    self_ref[...] = grad_ref[0:F]
+    neigh_ref[...] = grad_ref[F : 2 * F]
+    out_ref[...] = bias_ref[...]
 
 
 def per_device(source_feats, neighbours, degree, counts, upstream, preact):
@@ -270,7 +279,7 @@
             pltpu.VMEM((24, 128), f32),
             dma((5,)),
             dma((C, 4)), dma((C, 4)), dma((C, 4)), dma((C, 4)), dma((C, 8)), dma((C, 8)),
-            dma(()), dma(()), dma(()), dma(()), dma(()),
+            dma(()), dma(()), dma(()), dma(()), dma(()), pltpu.SemaphoreType.REGULAR((NY // 2 + 1,)),
         ],
         compiler_params=pltpu.CompilerParams(collective_id=0, has_side_effects=True, vmem_limit_bytes=60 << 20),
         name="sage_grads",
@@ -278,9 +287,8 @@
     own, neigh, bias = pl.pallas_call(
         place,
         out_shape=(jax.ShapeDtypeStruct((F, H), f32), jax.ShapeDtypeStruct((F, H), f32), jax.ShapeDtypeStruct((8, 128), f32)),
-        in_specs=[any_, any_],
-        out_specs=(any_, any_, any_),
-        scratch_shapes=[dma((3,))],
+        in_specs=[vmem, vmem],
+        out_specs=(vmem, vmem, vmem),
         compiler_params=pltpu.CompilerParams(vmem_limit_bytes=60 << 20),
         name="place",
     )(grad, bias)

time: 76.9 us -> 62 us (0.81)
  Pallas kernels: 75.5 us -> 60.6 us
    pallas_call x1, Pallas kernels: 13.2 us -> 1.76 us  [per_device(): pl.pallas_call(place, out_shape=(jax.ShapeDtypeStruct((F, H), f32), jax.S...]
    pallas_call x1, Pallas kernels: 62.3 us -> 58.8 us  [per_device(): pl.pallas_call(kernel, out_shape=(jax.ShapeDtypeStruct((2 * F, H), f32),...]
where the time goes in v3:
time: 62 us; the launch traced here: 61.9 us
  Pallas kernels  60.6 us (98%)
  between operations  1.29 us (2%)
    pallas_call x1, Pallas kernels, per_device(): pl.pallas_call(kernel, out_shape=(jax.ShapeDtypeStruct((2 * F, H), f32),...  58.8 us
    pallas_call x1, Pallas kernels, per_device(): pl.pallas_call(place, out_shape=(jax.ShapeDtypeStruct((F, H), f32), jax.S...  1.76 us

profile of v3, /device:TPU:1, one launch (start us, length us, event | category | flops | bytes accessed | tf_op | source)
XLA Modules:
  0.0 61.9 jit_solution(7584145098851274296)
XLA Ops:
  1.3 58.8 %sage_grads.1 = (f32[96,1024]{1,0:T(8,128)}, f32[8,128]{1,0:T(8,128)}) custom-call(bf16[48,4096]{1,0:T(8,128)(2,1)} %src_hbm.1, s32[25,2048]{1,0:T(8,128)} %bitcast.3, s32[1,2048]{1,0:T(1,128)} %bitcast.4, s32[1]{0:T(128)S(6)} %copy.9.counts_ref, bf16[128,1024]{1,0:T(8,128)(2,1)} %up_hbm.1, bf16[128,1024]{1,0:T(8,128)(2,1)} %pre_hbm.1), custom_call_target="tpu_custom_call" | custom-call | tf_op jit(solution)/shard_map/sage_grads/pallas_call | solution.py:259
  60.1 1.8 %place.1 = (f32[48,1024]{1,0:T(8,128)}, f32[48,1024]{1,0:T(8,128)}, f32[8,128]{1,0:T(8,128)}) custom-call(f32[96,1024]{1,0:T(8,128)} %get-tuple-element.8.grad_ref, f32[8,128]{1,0:T(8,128)} %get-tuple-element.9.bias_ref), custom_call_target="tpu_custom_call" | custom-call | tf_op jit(solution)/shard_map/place/pallas_call | solution.py:287

commit v4 on v3

--- a/solution.py
+++ b/solution.py
@@ -124,35 +124,41 @@
             src_ref=ref, dst_ref=ref, send_sem=send_sem, recv_sem=recv_sem, device_id=to, device_id_type=MESH
         )
 
-    def up(q, s, slot, rows):
-        return send(dz.at[q, slot, rows], up_send.at[q, s], up_recv.at[q, s], (dp, above))
-
-    def dn(q, s, slot, rows):
-        return send(dz.at[q, slot, rows], dn_send.at[q, s], dn_recv.at[q, s], (dp, below))
+    halves = pl.ds(0, ROWS // 2), pl.ds(ROWS // 2, ROWS // 2)
+
+    def up(q, s, far, slot):
+        n = q * 8 + s * 2 + far
+        return send(dz.at[q, slot, halves[1 - far]], up_send.at[n], up_recv.at[n], (dp, above))
+
+    def dn(q, s, far, slot):
+        n = q * 8 + s * 2 + far
+        return send(dz.at[q, slot, halves[far]], dn_send.at[n], dn_recv.at[n], (dp, below))
 
     def sib(q, i, slot):
         return send(dz.at[q, slot], sib_send.at[q, i], sib_recv.at[q, i], (dp, sibling))
 
-    whole, low, high = pl.ds(0, ROWS), pl.ds(0, ROWS // 2), pl.ds(ROWS // 2, ROWS // 2)
+    for far in (1, 0):
+        for q in range(C):
+            up(q, 0, far, col).start()
+            dn(q, 0, far, col).start()
     for q in range(C):
-        up(q, 0, col, whole).start()
-        dn(q, 0, col, whole).start()
         sib(q, 0, col).start()
 
-    def serve(s, q):
-        from_below = (z + NZ - s) % NZ * 2 + core
-        from_above = (z + s) % NZ * 2 + core
-        if s == 4:
-            up(q, s - 1, from_below, low).wait_recv()
-            dn(q, s - 1, from_below, high).wait_recv()
+    def serve(q, s, far):
+        from_below = (z + NZ - 1 - s) % NZ * 2 + core
+        from_above = (z + 1 + s) % NZ * 2 + core
+        onward = s < 2 + far
+        up(q, s, far, from_below).wait_recv()
+        if onward:
+            up(q, s + 1, far, from_below).start()
+        dn(q, s, far, from_above).wait_recv()
+        if onward:
+            dn(q, s + 1, far, from_above).start()
+        if s == 3:
             sib(q, 7, from_below).start()
-            return
-        up(q, s - 1, from_below, whole).wait_recv()
-        up(q, s, from_below, whole if s < 3 else low).start()
-        dn(q, s - 1, from_above, whole).wait_recv()
-        dn(q, s, from_above, whole if s < 3 else high).start()
-        sib(q, s, from_below).start()
-        sib(q, 3 + s, from_above).start()
+        elif not far:
+            sib(q, s + 1, from_below).start()
+            sib(q, s + 4, from_above).start()
 
     def add(dz_, i):
         at = (z + NZ + dz_) % NZ
@@ -173,7 +179,7 @@
         aggregate_block(i, src_s, hi_s, lo_s, tal, agg_s)
         for at, n in ((1, 0), (4, 1), (6, 2)):
             pl.when(i == at)(lambda n=n: hear(n))
-        for at, turn in ((3, (1, 0)), (4, (1, 1)), (7, (2, 0))):
+        for at, turn in ((3, (0, 0, 1)), (4, (1, 0, 1)), (5, (0, 0, 0)), (6, (1, 0, 0)), (7, (0, 1, 1))):
             pl.when(i == at)(lambda turn=turn: serve(*turn))
         return 0
 
@@ -186,19 +192,23 @@
         lhs[F : 2 * F, at] = (total[0:F] / jnp.maximum(deg_s[:, at], 1).astype(jnp.float32)).astype(jnp.bfloat16)
     lhs[2 * F : 2 * F + 16] = jnp.ones((16, T), jnp.bfloat16)
 
-    serve(2, 1)
+    serve(1, 1, 1)
     hear(3)
     add(0, 0)
+    serve(0, 1, 0)
+    serve(1, 1, 0)
     add(-1, 1)
     add(1, 4)
-    serve(3, 0)
-    serve(3, 1)
+    serve(0, 2, 1)
+    serve(1, 2, 1)
     add(-2, 2)
     add(2, 5)
-    serve(4, 0)
-    serve(4, 1)
+    serve(0, 2, 0)
+    serve(1, 2, 0)
     add(-3, 3)
     add(3, 6)
+    serve(0, 3, 1)
+    serve(1, 3, 1)
     add(4, 7)
 
     bias = jnp.concatenate([acc[2 * F : 2 * F + 1, b * 128 : (b + 1) * 128] for b in range(8)], axis=0)
@@ -208,42 +218,58 @@
             part[a * 8 + b] = jnp.concatenate([rows, bias], axis=0).astype(jnp.bfloat16)
 
     hear(4)
-    for p in PEERS:
-        pltpu.make_async_remote_copy(
-            src_ref=part.at[peer(*p)], dst_ref=rs.at[dp], send_sem=rs_send, recv_sem=rs_recv,
-            device_id=(peer(*p), col), device_id_type=MESH,
-        ).start()
-    rs[dp] = part[dp]
-    pltpu.make_async_copy(rs.at[pl.ds(0, NP)], rs.at[pl.ds(0, NP)], rs_recv).wait()
+
+    def scatter(n):
+        half = pl.ds(n * 16, 16)
+        for p in PEERS:
+            pltpu.make_async_remote_copy(
+                src_ref=part.at[peer(*p), half], dst_ref=rs.at[n, dp], send_sem=rs_send.at[n], recv_sem=rs_recv.at[n],
+                device_id=(peer(*p), col), device_id_type=MESH,
+            ).start()
+        rs[n, dp] = part[dp, n * 16 : n * 16 + 16]
 
     scale = jnp.float32(1.0) / jnp.sqrt(jnp.float32(T * NDP))
-    total = rs[0].astype(jnp.float32)
-    for d in range(1, NDP):
-        total += rs[d].astype(jnp.float32)
-    total *= scale
-    mine[...] = total[0:24]
-    bias_ref[...] = total[24:32]
-
-    rows, cols = pl.ds(pl.multiple_of(dp // 8 * 24, 8), 24), pl.ds(pl.multiple_of(dp % 8 * 128, 128), 128)
-    for p in PEERS:
-        pltpu.make_async_remote_copy(
-            src_ref=mine, dst_ref=grad_ref.at[rows, cols], send_sem=ag_send, recv_sem=ag_recv,
-            device_id=(peer(*p), col), device_id_type=MESH,
-        ).start()
-    own = pltpu.make_async_copy(mine, grad_ref.at[rows, cols], own_sem)
-    own.start()
+    cols = pl.ds(pl.multiple_of(dp % 8 * 128, 128), 128)
+
+    def spread(n):
+        every = rs.at[n, pl.ds(0, NP)]
+        pltpu.make_async_copy(every, every, rs_recv.at[n]).wait()
+        total = rs[n, 0].astype(jnp.float32)
+        for d in range(1, NDP):
+            total += rs[n, d].astype(jnp.float32)
+        total *= scale
+        size = 16 - 8 * n
+        rows = pl.ds(pl.multiple_of(dp // 8 * 24 + n * 16, 8), size)
+        mine[n] = total
+        for p in PEERS:
+            pltpu.make_async_remote_copy(
+                src_ref=mine.at[n, pl.ds(0, size)], dst_ref=grad_ref.at[rows, cols], send_sem=ag_send.at[n],
+                recv_sem=ag_recv.at[n], device_id=(peer(*p), col), device_id_type=MESH,
+            ).start()
+        own = pltpu.make_async_copy(mine.at[n, pl.ds(0, size)], grad_ref.at[rows, cols], own_sem.at[n])
+        own.start()
+        return own
+
+    scatter(0)
+    scatter(1)
+    owns = [spread(0), spread(1)]
+    bias_ref[...] = mine[1, 8:16]
 
     for q in range(C):
         for s in range(4):
-            up(q, s, col, whole if s < 3 else low).wait_send()
-            dn(q, s, col, whole if s < 3 else high).wait_send()
+            for far in (1, 0) if s < 3 else (1,):
+                up(q, s, far, col).wait_send()
+                dn(q, s, far, col).wait_send()
         for i in range(8):
             sib(q, i, col).wait_send()
-    pltpu.make_async_copy(part.at[pl.ds(0, NP)], part.at[pl.ds(0, NP)], rs_send).wait()
-    own.wait()
-    every = agg_s.at[pl.ds(0, NP * 24)]
-    pltpu.make_async_copy(every, every, ag_send).wait()
-    pltpu.make_async_copy(every, every, ag_recv).wait()
+    for n in range(2):
+        sent, every = rs.at[n, pl.ds(0, NP)], agg_s.at[pl.ds(0, NP * (16 - 8 * n))]
+        pltpu.make_async_copy(sent, sent, rs_send.at[n]).wait()
+        owns[n].wait()
+        pltpu.make_async_copy(every, every, ag_send.at[n]).wait()
+    for n in range(2):
+        every = agg_s.at[pl.ds(0, NP * (16 - 8 * n))]
+        pltpu.make_async_copy(every, every, ag_recv.at[n]).wait()
 
 
 def place(grad_ref, bias_ref, self_ref, neigh_ref, out_ref):
@@ -275,11 +301,11 @@
             pltpu.VMEM((C, NCOL, ROWS, W), bf16),
             pltpu.VMEM((2 * F + 16, H), f32),
             pltpu.VMEM((NDP, 32, 128), bf16),
-            pltpu.VMEM((NDP, 32, 128), bf16),
-            pltpu.VMEM((24, 128), f32),
+            pltpu.VMEM((2, NDP, 16, 128), bf16),
+            pltpu.VMEM((2, 16, 128), f32),
             dma((5,)),
-            dma((C, 4)), dma((C, 4)), dma((C, 4)), dma((C, 4)), dma((C, 8)), dma((C, 8)),
-            dma(()), dma(()), dma(()), dma(()), dma(()), pltpu.SemaphoreType.REGULAR((NY // 2 + 1,)),
+            dma((C * 8,)), dma((C * 8,)), dma((C * 8,)), dma((C * 8,)), dma((C, 8)), dma((C, 8)),
+            dma((2,)), dma((2,)), dma((2,)), dma((2,)), dma((2,)), pltpu.SemaphoreType.REGULAR((NY // 2 + 1,)),
         ],
         compiler_params=pltpu.CompilerParams(collective_id=0, has_side_effects=True, vmem_limit_bytes=60 << 20),
         name="sage_grads",

time: 62 us -> 60.7 us (0.979)
  Pallas kernels: 60.6 us -> 59.2 us
    pallas_call x1, Pallas kernels: 58.8 us -> 57.5 us  [per_device(): pl.pallas_call(kernel, out_shape=(jax.ShapeDtypeStruct((2 * F, H), f32),...]
where the time goes in v4:
time: 60.7 us; the launch traced here: 60.5 us
  Pallas kernels  59.2 us (98%)
  between operations  1.29 us (2%)
    pallas_call x1, Pallas kernels, per_device(): pl.pallas_call(kernel, out_shape=(jax.ShapeDtypeStruct((2 * F, H), f32),...  57.5 us
    pallas_call x1, Pallas kernels, per_device(): pl.pallas_call(place, out_shape=(jax.ShapeDtypeStruct((F, H), f32), jax.S...  1.76 us

profile of v4, /device:TPU:1, one launch (start us, length us, event | category | flops | bytes accessed | tf_op | source)
XLA Modules:
  0.0 60.5 jit_solution(8258835886289550047)
XLA Ops:
  1.3 57.5 %sage_grads.1 = (f32[96,1024]{1,0:T(8,128)}, f32[8,128]{1,0:T(8,128)}) custom-call(bf16[48,4096]{1,0:T(8,128)(2,1)} %src_hbm.1, s32[25,2048]{1,0:T(8,128)} %bitcast.3, s32[1,2048]{1,0:T(1,128)} %bitcast.4, s32[1]{0:T(128)S(6)} %copy.9.counts_ref, bf16[128,1024]{1,0:T(8,128)(2,1)} %up_hbm.1, bf16[128,1024]{1,0:T(8,128)(2,1)} %pre_hbm.1), custom_call_target="tpu_custom_call" | custom-call | tf_op jit(solution)/shard_map/sage_grads/pallas_call | solution.py:285
  58.8 1.8 %place.1 = (f32[48,1024]{1,0:T(8,128)}, f32[48,1024]{1,0:T(8,128)}, f32[8,128]{1,0:T(8,128)}) custom-call(f32[96,1024]{1,0:T(8,128)} %get-tuple-element.8.grad_ref, f32[8,128]{1,0:T(8,128)} %get-tuple-element.9.bias_ref), custom_call_target="tpu_custom_call" | custom-call | tf_op jit(solution)/shard_map/place/pallas_call | solution.py:313

commit v5 on v4

--- a/solution.py
+++ b/solution.py
@@ -70,8 +70,8 @@
 def kernel(
     src_hbm, nbr_hbm, deg_hbm, counts_ref, up_hbm, pre_hbm,
     grad_ref, bias_ref,
-    src_s, nbr_s, deg_s, up_s, pre_s, hi_s, lo_s, tal, agg_s, lhs, dz, acc, part, rs, mine,
-    load_sem, up_send, up_recv, dn_send, dn_recv, sib_send, sib_recv, rs_send, rs_recv, ag_send, ag_recv, own_sem, news,
+    src_s, nbr_s, deg_s, up_s, pre_s, hi_s, lo_s, tal, agg_s, lhs, dz, acc, part, rs, mine, stage,
+    load_sem, up_send, up_recv, dn_send, dn_recv, sib_send, sib_recv, rs_send, rs_recv, y_send, y_recv, x_send, x_recv, own_sem, news,
 ):
     dp, col = lax.axis_index("dp"), lax.axis_index("col")
     y, x, z, core = dp // NX, dp % NX, col // 2, col % 2
@@ -177,10 +177,10 @@
 
     def step(i, _):
         aggregate_block(i, src_s, hi_s, lo_s, tal, agg_s)
-        for at, n in ((1, 0), (4, 1), (6, 2)):
-            pl.when(i == at)(lambda n=n: hear(n))
         for at, turn in ((3, (0, 0, 1)), (4, (1, 0, 1)), (5, (0, 0, 0)), (6, (1, 0, 0)), (7, (0, 1, 1))):
             pl.when(i == at)(lambda turn=turn: serve(*turn))
+        for at, n in ((3, 0), (5, 1), (7, 2)):
+            pl.when(i == at)(lambda n=n: hear(n))
         return 0
 
     lax.fori_loop(0, 8, step, 0)
@@ -229,7 +229,24 @@
         rs[n, dp] = part[dp, n * 16 : n * 16 + 16]
 
     scale = jnp.float32(1.0) / jnp.sqrt(jnp.float32(T * NDP))
-    cols = pl.ds(pl.multiple_of(dp % 8 * 128, 128), 128)
+
+    def tile(owner, n):
+        rows = pl.ds(pl.multiple_of(owner // 8 * 24 + n * 16, 8), 16 - 8 * n)
+        return grad_ref.at[rows, pl.ds(pl.multiple_of(owner % 8 * 128, 128), 128)]
+
+    def along_x(ref, owner, n):
+        for dx in (2, 1, 3):
+            pltpu.make_async_remote_copy(
+                src_ref=ref, dst_ref=tile(owner, n), send_sem=x_send.at[n], recv_sem=x_recv.at[n],
+                device_id=(peer(0, dx), col), device_id_type=MESH,
+            ).start()
+        pltpu.make_async_copy(ref, tile(owner, n), own_sem.at[n]).start()
+
+    def along_y(n, dy):
+        return pltpu.make_async_remote_copy(
+            src_ref=mine.at[n, pl.ds(0, 16 - 8 * n)], dst_ref=stage.at[n, dy, pl.ds(0, 16 - 8 * n)],
+            send_sem=y_send.at[n], recv_sem=y_recv.at[n * NY + dy], device_id=(peer(dy, 0), col), device_id_type=MESH,
+        )
 
     def spread(n):
         every = rs.at[n, pl.ds(0, NP)]
@@ -237,22 +254,22 @@
         total = rs[n, 0].astype(jnp.float32)
         for d in range(1, NDP):
             total += rs[n, d].astype(jnp.float32)
-        total *= scale
-        size = 16 - 8 * n
-        rows = pl.ds(pl.multiple_of(dp // 8 * 24 + n * 16, 8), size)
-        mine[n] = total
-        for p in PEERS:
-            pltpu.make_async_remote_copy(
-                src_ref=mine.at[n, pl.ds(0, size)], dst_ref=grad_ref.at[rows, cols], send_sem=ag_send.at[n],
-                recv_sem=ag_recv.at[n], device_id=(peer(*p), col), device_id_type=MESH,
-            ).start()
-        own = pltpu.make_async_copy(mine.at[n, pl.ds(0, size)], grad_ref.at[rows, cols], own_sem.at[n])
-        own.start()
-        return own
+        mine[n] = total * scale
+        for dy in (4, 3, 5, 2, 6, 1, 7):
+            along_y(n, dy).start()
+        along_x(mine.at[n, pl.ds(0, 16 - 8 * n)], dp, n)
+
+    def pass_on(n):
+        for dy in (1, 7, 2, 6, 3, 5, 4):
+            along_y(n, dy).wait_recv()
+            along_x(stage.at[n, dy, pl.ds(0, 16 - 8 * n)], peer(NY - dy, 0), n)
 
     scatter(0)
     scatter(1)
-    owns = [spread(0), spread(1)]
+    spread(0)
+    spread(1)
+    pass_on(0)
+    pass_on(1)
     bias_ref[...] = mine[1, 8:16]
 
     for q in range(C):
@@ -262,14 +279,14 @@
                 dn(q, s, far, col).wait_send()
         for i in range(8):
             sib(q, i, col).wait_send()
+    def as_many(tiles, n):
+        return agg_s.at[pl.ds(0, tiles * (16 - 8 * n))]
+
     for n in range(2):
-        sent, every = rs.at[n, pl.ds(0, NP)], agg_s.at[pl.ds(0, NP * (16 - 8 * n))]
+        sent = rs.at[n, pl.ds(0, NP)]
         pltpu.make_async_copy(sent, sent, rs_send.at[n]).wait()
-        owns[n].wait()
-        pltpu.make_async_copy(every, every, ag_send.at[n]).wait()
-    for n in range(2):
-        every = agg_s.at[pl.ds(0, NP * (16 - 8 * n))]
-        pltpu.make_async_copy(every, every, ag_recv.at[n]).wait()
+        for sem, tiles in ((y_send, NY - 1), (own_sem, NY), (x_send, NY * (NX - 1)), (x_recv, NY * (NX - 1))):
+            pltpu.make_async_copy(as_many(tiles, n), as_many(tiles, n), sem.at[n]).wait()
 
 
 def place(grad_ref, bias_ref, self_ref, neigh_ref, out_ref):
@@ -303,9 +320,10 @@
             pltpu.VMEM((NDP, 32, 128), bf16),
             pltpu.VMEM((2, NDP, 16, 128), bf16),
             pltpu.VMEM((2, 16, 128), f32),
+            pltpu.VMEM((2, NY, 16, 128), f32),
             dma((5,)),
             dma((C * 8,)), dma((C * 8,)), dma((C * 8,)), dma((C * 8,)), dma((C, 8)), dma((C, 8)),
-            dma((2,)), dma((2,)), dma((2,)), dma((2,)), dma((2,)), pltpu.SemaphoreType.REGULAR((NY // 2 + 1,)),
+            dma((2,)), dma((2,)), dma((2,)), dma((2 * NY,)), dma((2,)), dma((2,)), dma((2,)), pltpu.SemaphoreType.REGULAR((NY // 2 + 1,)),
         ],
         compiler_params=pltpu.CompilerParams(collective_id=0, has_side_effects=True, vmem_limit_bytes=60 << 20),
         name="sage_grads",

time: 60.7 us -> 59 us (0.972)
  Pallas kernels: 59.2 us -> 57.6 us
    pallas_call x1, Pallas kernels: 57.5 us -> 55.8 us  [per_device(): pl.pallas_call(kernel, out_shape=(jax.ShapeDtypeStruct((2 * F, H), f32),...]
where the time goes in v5:
time: 59 us; the launch traced here: 58.8 us
  Pallas kernels  57.6 us (98%)
  between operations  1.29 us (2%)
    pallas_call x1, Pallas kernels, per_device(): pl.pallas_call(kernel, out_shape=(jax.ShapeDtypeStruct((2 * F, H), f32),...  55.8 us
    pallas_call x1, Pallas kernels, per_device(): pl.pallas_call(place, out_shape=(jax.ShapeDtypeStruct((F, H), f32), jax.S...  1.76 us

profile of v5, /device:TPU:1, one launch (start us, length us, event | category | flops | bytes accessed | tf_op | source)
XLA Modules:
  0.0 58.8 jit_solution(17610334849245994476)
XLA Ops:
  1.3 55.8 %sage_grads.1 = (f32[96,1024]{1,0:T(8,128)}, f32[8,128]{1,0:T(8,128)}) custom-call(bf16[48,4096]{1,0:T(8,128)(2,1)} %src_hbm.1, s32[25,2048]{1,0:T(8,128)} %bitcast.3, s32[1,2048]{1,0:T(1,128)} %bitcast.4, s32[1]{0:T(128)S(6)} %copy.9.counts_ref, bf16[128,1024]{1,0:T(8,128)(2,1)} %up_hbm.1, bf16[128,1024]{1,0:T(8,128)(2,1)} %pre_hbm.1), custom_call_target="tpu_custom_call" | custom-call | tf_op jit(solution)/shard_map/sage_grads/pallas_call | solution.py:302
  57.1 1.8 %place.1 = (f32[48,1024]{1,0:T(8,128)}, f32[48,1024]{1,0:T(8,128)}, f32[8,128]{1,0:T(8,128)}) custom-call(f32[96,1024]{1,0:T(8,128)} %get-tuple-element.8.grad_ref, f32[8,128]{1,0:T(8,128)} %get-tuple-element.9.bias_ref), custom_call_target="tpu_custom_call" | custom-call | tf_op jit(solution)/shard_map/place/pallas_call | solution.py:331

commit v6 on v5

--- a/solution.py
+++ b/solution.py
@@ -160,12 +160,11 @@
             sib(q, s + 1, from_below).start()
             sib(q, s + 4, from_above).start()
 
-    def add(dz_, i):
+    def add(dz_, i, chunks=range(C)):
         at = (z + NZ + dz_) % NZ
-        for q in range(C):
+        rows = lhs[:, pl.ds(pl.multiple_of(at * 2 * ROWS, 2 * ROWS), 2 * ROWS)]
+        for q in chunks:
             sib(q, i, at * 2 + 1 - core).wait_recv()
-        rows = lhs[:, pl.ds(pl.multiple_of(at * 2 * ROWS, 2 * ROWS), 2 * ROWS)]
-        for q in range(C):
             new = jnp.dot(rows, dz[q, pl.ds(at * 2, 2)].reshape(2 * ROWS, W), preferred_element_type=jnp.float32)
             here = slice(q * W, (q + 1) * W)
             acc[:, here] = new if dz_ == 0 else acc[:, here] + new
@@ -177,7 +176,7 @@
 
     def step(i, _):
         aggregate_block(i, src_s, hi_s, lo_s, tal, agg_s)
-        for at, turn in ((3, (0, 0, 1)), (4, (1, 0, 1)), (5, (0, 0, 0)), (6, (1, 0, 0)), (7, (0, 1, 1))):
+        for at, turn in ((2, (0, 0, 1)), (3, (1, 0, 1)), (4, (0, 0, 0)), (5, (1, 0, 0)), (6, (0, 1, 1)), (7, (1, 1, 1))):
             pl.when(i == at)(lambda turn=turn: serve(*turn))
         for at, n in ((3, 0), (5, 1), (7, 2)):
             pl.when(i == at)(lambda n=n: hear(n))
@@ -192,7 +191,6 @@
         lhs[F : 2 * F, at] = (total[0:F] / jnp.maximum(deg_s[:, at], 1).astype(jnp.float32)).astype(jnp.bfloat16)
     lhs[2 * F : 2 * F + 16] = jnp.ones((16, T), jnp.bfloat16)
 
-    serve(1, 1, 1)
     hear(3)
     add(0, 0)
     serve(0, 1, 0)
@@ -207,15 +205,22 @@
     serve(1, 2, 0)
     add(-3, 3)
     add(3, 6)
-    serve(0, 3, 1)
-    serve(1, 3, 1)
-    add(4, 7)
-
+
+    for q in range(C):
+        serve(q, 3, 1)
+        add(4, 7, (q,))
+        for b in range(q * 8 // C, (q + 1) * 8 // C):
+            at = slice(b * 128, (b + 1) * 128)
+            for a in range(4):
+                part[a * 8 + b, 0:16] = acc[a * 24 : a * 24 + 16, at].astype(jnp.bfloat16)
     bias = jnp.concatenate([acc[2 * F : 2 * F + 1, b * 128 : (b + 1) * 128] for b in range(8)], axis=0)
-    for a in range(4):
+
+    def finish_part():
         for b in range(8):
-            rows = acc[a * 24 : a * 24 + 24, b * 128 : (b + 1) * 128]
-            part[a * 8 + b] = jnp.concatenate([rows, bias], axis=0).astype(jnp.bfloat16)
+            at = slice(b * 128, (b + 1) * 128)
+            for a in range(4):
+                rows = acc[a * 24 + 16 : a * 24 + 24, at]
+                part[a * 8 + b, 16:32] = jnp.concatenate([rows, bias], axis=0).astype(jnp.bfloat16)
 
     hear(4)
 
@@ -255,9 +260,17 @@
         for d in range(1, NDP):
             total += rs[n, d].astype(jnp.float32)
         mine[n] = total * scale
+        if n == 1:
+            for p in PEERS:
+                pltpu.make_async_remote_copy(
+                    src_ref=mine.at[n, pl.ds(0, 8)], dst_ref=tile(dp, n), send_sem=x_send.at[n], recv_sem=x_recv.at[n],
+                    device_id=(peer(*p), col), device_id_type=MESH,
+                ).start()
+            pltpu.make_async_copy(mine.at[n, pl.ds(0, 8)], tile(dp, n), own_sem.at[n]).start()
+            return
         for dy in (4, 3, 5, 2, 6, 1, 7):
             along_y(n, dy).start()
-        along_x(mine.at[n, pl.ds(0, 16 - 8 * n)], dp, n)
+        along_x(mine.at[n, pl.ds(0, 16)], dp, n)
 
     def pass_on(n):
         for dy in (1, 7, 2, 6, 3, 5, 4):
@@ -265,11 +278,11 @@
             along_x(stage.at[n, dy, pl.ds(0, 16 - 8 * n)], peer(NY - dy, 0), n)
 
     scatter(0)
+    finish_part()
     scatter(1)
     spread(0)
     spread(1)
     pass_on(0)
-    pass_on(1)
     bias_ref[...] = mine[1, 8:16]
 
     for q in range(C):
@@ -285,7 +298,9 @@
     for n in range(2):
         sent = rs.at[n, pl.ds(0, NP)]
         pltpu.make_async_copy(sent, sent, rs_send.at[n]).wait()
-        for sem, tiles in ((y_send, NY - 1), (own_sem, NY), (x_send, NY * (NX - 1)), (x_recv, NY * (NX - 1))):
+        relayed = ((y_send, NY - 1), (own_sem, NY), (x_send, NY * (NX - 1)), (x_recv, NY * (NX - 1)))
+        direct = ((own_sem, 1), (x_send, NP), (x_recv, NP))
+        for sem, tiles in direct if n else relayed:
             pltpu.make_async_copy(as_many(tiles, n), as_many(tiles, n), sem.at[n]).wait()
 
 

time: 59 us -> 57 us (0.966)
  Pallas kernels: 57.6 us -> 55.6 us
    pallas_call x1, Pallas kernels: 55.8 us -> 53.8 us  [per_device(): pl.pallas_call(kernel, out_shape=(jax.ShapeDtypeStruct((2 * F, H), f32),...]
where the time goes in v6:
time: 57 us; the launch traced here: 56.9 us
  Pallas kernels  55.6 us (98%)
  between operations  1.29 us (2%)
    pallas_call x1, Pallas kernels, per_device(): pl.pallas_call(kernel, out_shape=(jax.ShapeDtypeStruct((2 * F, H), f32),...  53.8 us
    pallas_call x1, Pallas kernels, per_device(): pl.pallas_call(place, out_shape=(jax.ShapeDtypeStruct((F, H), f32), jax.S...  1.76 us

profile of v6, /device:TPU:1, one launch (start us, length us, event | category | flops | bytes accessed | tf_op | source)
XLA Modules:
  0.0 56.9 jit_solution(16951905668137810013)
XLA Ops:
  1.3 53.8 %sage_grads.1 = (f32[96,1024]{1,0:T(8,128)}, f32[8,128]{1,0:T(8,128)}) custom-call(bf16[48,4096]{1,0:T(8,128)(2,1)} %src_hbm.1, s32[25,2048]{1,0:T(8,128)} %bitcast.3, s32[1,2048]{1,0:T(1,128)} %bitcast.4, s32[1]{0:T(128)S(6)} %copy.9.counts_ref, bf16[128,1024]{1,0:T(8,128)(2,1)} %up_hbm.1, bf16[128,1024]{1,0:T(8,128)(2,1)} %pre_hbm.1), custom_call_target="tpu_custom_call" | custom-call | tf_op jit(solution)/shard_map/sage_grads/pallas_call | solution.py:317
  55.1 1.8 %place.1 = (f32[48,1024]{1,0:T(8,128)}, f32[48,1024]{1,0:T(8,128)}, f32[8,128]{1,0:T(8,128)}) custom-call(f32[96,1024]{1,0:T(8,128)} %get-tuple-element.8.grad_ref, f32[8,128]{1,0:T(8,128)} %get-tuple-element.9.bias_ref), custom_call_target="tpu_custom_call" | custom-call | tf_op jit(solution)/shard_map/place/pallas_call | solution.py:346

commit v7 on v6

--- a/solution.py
+++ b/solution.py
@@ -71,7 +71,7 @@
     src_hbm, nbr_hbm, deg_hbm, counts_ref, up_hbm, pre_hbm,
     grad_ref, bias_ref,
     src_s, nbr_s, deg_s, up_s, pre_s, hi_s, lo_s, tal, agg_s, lhs, dz, acc, part, rs, mine, stage,
-    load_sem, up_send, up_recv, dn_send, dn_recv, sib_send, sib_recv, rs_send, rs_recv, y_send, y_recv, x_send, x_recv, own_sem, news,
+    load_sem, up_send, up_recv, dn_send, dn_recv, sib_send, sib_recv, rs_send, rs_recv, y_send, y_recv, x_send, x_recv, own_sem, bias_sem, news,
 ):
     dp, col = lax.axis_index("dp"), lax.axis_index("col")
     y, x, z, core = dp // NX, dp % NX, col // 2, col % 2
@@ -267,6 +267,7 @@
                     device_id=(peer(*p), col), device_id_type=MESH,
                 ).start()
             pltpu.make_async_copy(mine.at[n, pl.ds(0, 8)], tile(dp, n), own_sem.at[n]).start()
+            pltpu.make_async_copy(mine.at[n, pl.ds(8, 8)], bias_ref, bias_sem).start()
             return
         for dy in (4, 3, 5, 2, 6, 1, 7):
             along_y(n, dy).start()
@@ -283,7 +284,6 @@
     spread(0)
     spread(1)
     pass_on(0)
-    bias_ref[...] = mine[1, 8:16]
 
     for q in range(C):
         for s in range(4):
@@ -295,6 +295,7 @@
     def as_many(tiles, n):
         return agg_s.at[pl.ds(0, tiles * (16 - 8 * n))]
 
+    pltpu.make_async_copy(mine.at[1, pl.ds(8, 8)], bias_ref, bias_sem).wait()
     for n in range(2):
         sent = rs.at[n, pl.ds(0, NP)]
         pltpu.make_async_copy(sent, sent, rs_send.at[n]).wait()
@@ -318,7 +319,7 @@
         kernel,
         out_shape=(jax.ShapeDtypeStruct((2 * F, H), f32), jax.ShapeDtypeStruct((8, 128), f32)),
         in_specs=[any_, any_, any_, pl.BlockSpec(memory_space=pltpu.SMEM), any_, any_],
-        out_specs=(any_, vmem),
+        out_specs=(any_, any_),
         scratch_shapes=[
             pltpu.VMEM((F, 4096), bf16),
             pltpu.VMEM((25, T), i32),
@@ -338,7 +339,7 @@
             pltpu.VMEM((2, NY, 16, 128), f32),
             dma((5,)),
             dma((C * 8,)), dma((C * 8,)), dma((C * 8,)), dma((C * 8,)), dma((C, 8)), dma((C, 8)),
-            dma((2,)), dma((2,)), dma((2,)), dma((2 * NY,)), dma((2,)), dma((2,)), dma((2,)), pltpu.SemaphoreType.REGULAR((NY // 2 + 1,)),
+            dma((2,)), dma((2,)), dma((2,)), dma((2 * NY,)), dma((2,)), dma((2,)), dma((2,)), dma(()), pltpu.SemaphoreType.REGULAR((NY // 2 + 1,)),
         ],
         compiler_params=pltpu.CompilerParams(collective_id=0, has_side_effects=True, vmem_limit_bytes=60 << 20),
         name="sage_grads",

time: 57 us -> 56.4 us (0.989)
  Pallas kernels: 55.6 us -> 55 us
    pallas_call x1, Pallas kernels: 53.8 us -> 53.2 us  [per_device(): pl.pallas_call(kernel, out_shape=(jax.ShapeDtypeStruct((2 * F, H), f32),...]
where the time goes in v7:
time: 56.4 us; the launch traced here: 56.3 us
  Pallas kernels  55 us (98%)
  between operations  1.29 us (2%)
    pallas_call x1, Pallas kernels, per_device(): pl.pallas_call(kernel, out_shape=(jax.ShapeDtypeStruct((2 * F, H), f32),...  53.2 us
    pallas_call x1, Pallas kernels, per_device(): pl.pallas_call(place, out_shape=(jax.ShapeDtypeStruct((F, H), f32), jax.S...  1.76 us

profile of v7, /device:TPU:1, one launch (start us, length us, event | category | flops | bytes accessed | tf_op | source)
XLA Modules:
  0.0 56.3 jit_solution(7965507448333221838)
XLA Ops:
  1.3 53.2 %sage_grads.1 = (f32[96,1024]{1,0:T(8,128)}, f32[8,128]{1,0:T(8,128)}) custom-call(bf16[48,4096]{1,0:T(8,128)(2,1)} %src_hbm.1, s32[25,2048]{1,0:T(8,128)} %bitcast.3, s32[1,2048]{1,0:T(1,128)} %bitcast.4, s32[1]{0:T(128)S(6)} %copy.9.counts_ref, bf16[128,1024]{1,0:T(8,128)(2,1)} %up_hbm.1, bf16[128,1024]{1,0:T(8,128)(2,1)} %pre_hbm.1), custom_call_target="tpu_custom_call" | custom-call | tf_op jit(solution)/shard_map/sage_grads/pallas_call | solution.py:318
  54.5 1.8 %place.1 = (f32[48,1024]{1,0:T(8,128)}, f32[48,1024]{1,0:T(8,128)}, f32[8,128]{1,0:T(8,128)}) custom-call(f32[96,1024]{1,0:T(8,128)} %get-tuple-element.8.grad_ref, f32[8,128]{1,0:T(8,128)} %get-tuple-element.9.bias_ref), custom_call_target="tpu_custom_call" | custom-call | tf_op jit(solution)/shard_map/place/pallas_call | solution.py:347

commit v8 on v7

--- a/solution.py
+++ b/solution.py
@@ -329,7 +329,7 @@
             pltpu.VMEM((256, 256), f32),
             pltpu.VMEM((256, 256), f32),
             pltpu.VMEM((16, 256, 256), bf16),
-            pltpu.VMEM((T, 128), f32),
+            pltpu.VMEM((T + 8, 128), f32),
             pltpu.VMEM((2 * F + 16, T), bf16),
             pltpu.VMEM((C, NCOL, ROWS, W), bf16),
             pltpu.VMEM((2 * F + 16, H), f32),

time: 56.4 us -> 56.4 us (level)
  no operation moved by 1% of the time
where the time goes in v8:
time: 56.4 us; the launch traced here: 56.3 us
  Pallas kernels  55 us (98%)
  between operations  1.29 us (2%)
    pallas_call x1, Pallas kernels, per_device(): pl.pallas_call(kernel, out_shape=(jax.ShapeDtypeStruct((2 * F, H), f32),...  53.2 us
    pallas_call x1, Pallas kernels, per_device(): pl.pallas_call(place, out_shape=(jax.ShapeDtypeStruct((F, H), f32), jax.S...  1.76 us

profile of v8, /device:TPU:1, one launch (start us, length us, event | category | flops | bytes accessed | tf_op | source)
XLA Modules:
  0.0 56.3 jit_solution(1848314901399903362)
XLA Ops:
  1.3 53.2 %sage_grads.1 = (f32[96,1024]{1,0:T(8,128)}, f32[8,128]{1,0:T(8,128)}) custom-call(bf16[48,4096]{1,0:T(8,128)(2,1)} %src_hbm.1, s32[25,2048]{1,0:T(8,128)} %bitcast.3, s32[1,2048]{1,0:T(1,128)} %bitcast.4, s32[1]{0:T(128)S(6)} %copy.9.counts_ref, bf16[128,1024]{1,0:T(8,128)(2,1)} %up_hbm.1, bf16[128,1024]{1,0:T(8,128)(2,1)} %pre_hbm.1), custom_call_target="tpu_custom_call" | custom-call | tf_op jit(solution)/shard_map/sage_grads/pallas_call | solution.py:318
  54.5 1.8 %place.1 = (f32[48,1024]{1,0:T(8,128)}, f32[48,1024]{1,0:T(8,128)}, f32[8,128]{1,0:T(8,128)}) custom-call(f32[96,1024]{1,0:T(8,128)} %get-tuple-element.8.grad_ref, f32[8,128]{1,0:T(8,128)} %get-tuple-element.9.bias_ref), custom_call_target="tpu_custom_call" | custom-call | tf_op jit(solution)/shard_map/place/pallas_call | solution.py:347
